TPU v7x, 32 devices: a whole 2x2x4 slice. The times are simulated.
32 devices in a mesh: row: 4 (over z), col: 8 (over y, x, core).
Axes of the slice: x: 2, y: 2, z: 4, core: 2. Of those that a mesh axis runs over, the one named last changes fastest.
Arguments:
- iterate: float32 [256, 16384], P('row', 'col'), may hold values from -6 to 6
- residual: float32 [256, 16384], P('row', 'col'), may hold values from -24 to 24
- direction: float32 [256, 16384], P('row', 'col'), may hold values from -24 to 24
- window_weight: float32 [16, 1024], P('row', 'col'), may hold values from 0.2 to 5
- freq_weight: float32 [32, 32], replicated, may hold values from 0.2 to 5
Outputs:
- new_iterate: float32 [256, 16384], P('row', 'col')
- new_residual: float32 [256, 16384], P('row', 'col')
- new_direction: float32 [256, 16384], P('row', 'col')
All inputs are finite; a program needn't handle non-finite values.
Results may differ from a plain program's by a relative error of at most 0.0003.
Values sent between devices are 32-bit elements; how exact they have to be, the bound alone decides.
A program may use at most 64 MiB of HBM per device.

v0:
```python
import jax
import jax.numpy as jnp
from jax import lax
from jax.sharding import PartitionSpec as P

precise = lax.Precision.HIGHEST
damping = 0.5


def passed_along(value, axis, steps):
    count = lax.axis_size(axis)
    leading, last = (max(0, -steps), min(count, count - steps))
    return lax.ppermute(value, axis, [(source, source + steps) for source in range(leading, last)])


def tables():
    positions = jnp.arange(32, dtype=jnp.float32)
    window = jnp.exp(-0.5 * ((positions - 15.5) / 8.0) ** 2)
    phases = 2.0 * jnp.pi * jnp.outer(positions, positions) / 32.0
    cos_part = jnp.cos(phases) * window[None, :] / jnp.sqrt(32.0)
    sin_part = -jnp.sin(phases) * window[None, :] / jnp.sqrt(32.0)
    column_table = jnp.concatenate([cos_part.T, sin_part.T], axis=1)
    cos_split = cos_part.reshape(32, 2, 16)
    sin_split = sin_part.reshape(32, 2, 16)
    upper = jnp.stack([cos_split, -sin_split], axis=-1)
    lower = jnp.stack([sin_split, cos_split], axis=-1)
    row_table = jnp.concatenate([upper, lower], axis=0).reshape(64, 64)
    return (column_table, row_table)


def analyze(region, column_table, row_table):
    win_rows = region.shape[0] // 16 - 1
    win_cols = region.shape[1] // 16 - 1
    blocks = region.reshape(win_rows + 1, 16, win_cols + 1, 16)
    section_one = jnp.einsum(
        "akbl,lp->akpb", blocks[:, :, :win_cols], column_table[:16], precision=precise
    )
    section_one = section_one + jnp.einsum(
        "akbl,lp->akpb", blocks[:, :, 1:], column_table[16:], precision=precise
    )
    section_one = section_one.reshape(win_rows + 1, 16, 2, 32, win_cols)
    paired = jnp.stack([section_one[:-1], section_one[1:]], axis=1).reshape(
        win_rows, 64, 32, win_cols
    )
    return jnp.einsum("tm,amvb->atvb", row_table, paired, precision=precise)


def weigh(coefficients, window_weight, freq_weight):
    doubled = jnp.concatenate([freq_weight, freq_weight], axis=0)
    return coefficients * doubled[None, :, :, None] * window_weight[:, None, None, :]


def synthesize(coefficients, column_table, row_table):
    win_rows = coefficients.shape[0]
    win_cols = coefficients.shape[3]
    spread = jnp.einsum("tm,atvb->amvb", row_table, coefficients, precision=precise)
    spread = spread.reshape(win_rows, 2, 16, 64, win_cols)
    stacked = jnp.pad(spread[:, 0], ((0, 1), (0, 0), (0, 0), (0, 0))) + jnp.pad(
        spread[:, 1], ((1, 0), (0, 0), (0, 0), (0, 0))
    )
    lower_piece = jnp.einsum("akpb,lp->akbl", stacked, column_table[:16], precision=precise)
    upper_piece = jnp.einsum("akpb,lp->akbl", stacked, column_table[16:], precision=precise)
    blocks = jnp.pad(lower_piece, ((0, 0), (0, 0), (0, 1), (0, 0))) + jnp.pad(
        upper_piece, ((0, 0), (0, 0), (1, 0), (0, 0))
    )
    return blocks.reshape(16 * (win_rows + 1), 16 * (win_cols + 1))


def per_device(iterate, residual, direction, window_weight, freq_weight):
    column_table, row_table = tables()
    height, breadth = direction.shape
    beside = passed_along(direction[:, :16], "col", -1)
    widened = jnp.concatenate([direction, beside], axis=1)
    below = passed_along(widened[:16], "row", -1)
    region = jnp.concatenate([widened, below], axis=0)
    coefficients = weigh(analyze(region, column_table, row_table), window_weight, freq_weight)
    spread = synthesize(coefficients, column_table, row_table)
    arrived_rows = passed_along(spread[height:], "row", 1)
    upper_rows = jnp.concatenate([spread[:16] + arrived_rows, spread[16:height]], axis=0)
    arrived_cols = passed_along(upper_rows[:, breadth:], "col", 1)
    synthesized = jnp.concatenate(
        [upper_rows[:, :16] + arrived_cols, upper_rows[:, 16:breadth]], axis=1
    )
    applied = synthesized + damping * direction
    norm_now, curvature, cross_term, image_norm = lax.psum(
        (
            jnp.sum(residual * residual),
            jnp.sum(direction * applied),
            jnp.sum(residual * applied),
            jnp.sum(applied * applied),
        ),
        ("row", "col"),
    )
    step_length = norm_now / curvature
    new_iterate = iterate + step_length * direction
    new_residual = residual - step_length * applied
    norm_next = norm_now - 2.0 * step_length * cross_term + step_length * step_length * image_norm
    new_direction = new_residual + norm_next / norm_now * direction
    return (new_iterate, new_residual, new_direction)


def solution(mesh):
    return jax.shard_map(
        per_device,
        mesh=mesh,
        in_specs=(P("row", "col"), P("row", "col"), P("row", "col"), P("row", "col"), P()),
        out_specs=(P("row", "col"), P("row", "col"), P("row", "col")),
        check_vma=False,
    )
```

profile of v0, /device:TPU:0, one launch (start us, length us, event | category | flops | bytes accessed | tf_op | source)
XLA Modules:
  0.0 116.1 jit_solution(17033692895881114362)
XLA Ops:
  0.6 0.8 slice.62
  1.4 1.3 %collective-permute-start = (f32[64,16]{1,0:T(8,128)S(1)}, f32[64,16]{1,0:T(8,128)S(1)}, u32[]{:S(2)}, u32[]{:S(2)}) collective-permute-start(f32[64,16]{1,0:T(8,128)S(1)} %slice.62), channel_id=1, source_target_pairs={{1,0},{2,1},{3,2},{4,3},{5,4},{6,5},{7,6},{9,8},{10,9},{11,10},{12... | collective-permute-start | bytes 12296 | tf_op jit(solution)/shard_map/ppermute | solution.py:13
  2.7 1.1 constant_dynamic-update-slice_fusion.1
  3.8 0.1 multiply_multiply_fusion.4
  3.9 0.1 fusion.26
  4.0 0.8 pad_maximum_fusion.2
  4.8 0.0 collective-permute-done
  4.9 1.3 %collective-permute-start.1 = (f32[16,2064]{1,0:T(8,128)S(1)}, f32[16,2064]{1,0:T(8,128)S(1)}, u32[]{:S(2)}, u32[]{:S(2)}) collective-permute-start(f32[16,2064]{1,0:T(8,128)S(1)} %slice.82), channel_id=1, source_target_pairs={{8,0},{16,8},{24,16},{9,1},{17,9},{25,17},{10,2},{18,10},{26,18},{... | collective-permute-start | bytes 396296 | tf_op jit(solution)/shard_map/ppermute | solution.py:13
  6.2 0.1 maximum_maximum_fusion
  6.3 0.1 copy.31
  6.3 0.1 fusion.25
  6.4 6.8 %collective-permute-done.1 = f32[16,2064]{1,0:T(8,128)S(1)} collective-permute-done((f32[16,2064]{1,0:T(8,128)S(1)}, f32[16,2064]{1,0:T(8,128)S(1)}, u32[]{:S(2)}, u32[]{:S(2)}) %collective-permute-start.1) | collective-permute-done | bytes 132128 | tf_op jit(solution)/shard_map/ppermute | solution.py:13
  13.2 3.3 %reshape.132 = f32[5,16,129,16]{3,2,1,0:T(8,128)} reshape(f32[80,2064]{1,0:T(8,128)S(1)} %pad_maximum_fusion) | data formatting | bytes 1320960 | tf_op jit(solution)/shard_map/reshape | solution.py:34
  16.5 8.1 %fusion = f32[64,5,16,128]{3,0,2,1:T(8,128)S(1)} fusion(f32[16,64,1,1]{1,0,3,2:T(8,128)S(1)} %fusion.25, f32[5,16,129,16]{3,2,1,0:T(8,128)} %reshape.132), kind=kOutput, calls=%fused_computation | convolution fusion | flops 125829120 | bytes 7868416 | tf_op jit(solution)/shard_map/akbl,lp->akpb/dot_general | solution.py:38
  24.6 0.0 copy-done
  24.6 5.8 %add_bitcast_fusion = f32[5,16,64,128]{3,2,1,0:T(8,128)S(1)} fusion(f32[64,5,16,128]{3,0,2,1:T(8,128)S(1)} %fusion, f32[5,16,129,16]{3,2,1,0:T(8,128)S(1)} %copy-done, f32[32,32]{1,0:T(8,128)S(1)} %get-tuple-element.24, f32[32,32]{1,0:T(8,128)S(1)} %get-tuple-element.25), kind=kOutput, calls=%fused_computation.12 | convolution fusion | flops 126485504 | bytes 10518528 | tf_op jit(solution)/shard_map/akbl,lp->akpb/dot_general | solution.py:35
  30.4 0.6 fusion.35
  31.0 1.2 %copy.29 = f32[4,1,16,2,32,128]{5,2,3,1,4,0:T(8,128)S(1)} copy(f32[4,1,16,2,32,128]{5,4,3,2,0,1:T(8,128)S(1)} %bitcast.49) | data formatting | bytes 4194304 | tf_op jit(solution)/shard_map/stack | solution.py:42
  32.3 1.2 %copy.30 = f32[4,1,16,2,32,128]{5,2,3,1,4,0:T(8,128)S(1)} copy(f32[4,1,16,2,32,128]{5,4,3,2,0,1:T(8,128)S(1)} %bitcast.48) | data formatting | bytes 4194304 | tf_op jit(solution)/shard_map/stack | solution.py:42
  33.5 0.0 copy-start.4
  33.5 4.2 %fusion.4 = f32[4,32,128,64,1,1]{2,3,5,4,1,0:T(8,128)S(1)} fusion(f32[4,1,16,2,32,128]{5,2,3,1,4,0:T(8,128)S(1)} %copy.30, f32[4,1,16,2,32,128]{5,2,3,1,4,0:T(8,128)S(1)} %copy.29, f32[64,2,16,2]{0,2,3,1:T(8,128)S(1)} %maximum_maximum_fusion), kind=kOutput, calls=%fused_computation.4 | convolution fusion | flops 806354944 | bytes 8404992 | tf_op jit(solution)/shard_map/tm,amvb->atvb/dot_general | solution.py:45
  37.7 0.0 copy-done.4
  37.7 4.4 %fusion.11 = f32[4,64,32,128]{3,1,2,0:T(8,128)S(1)} fusion(f32[64,64,1,1]{0,1,3,2:T(8,128)S(1)} %bitcast.50, f32[4,32,128,64,1,1]{2,3,5,4,1,0:T(8,128)S(1)} %fusion.4, f32[4,128]{1,0:T(4,128)S(1)} %copy-done.4, f32[64,32]{0,1:T(8,128)S(1)} %copy.31), kind=kOutput, calls=%fused_computation.13 | convolution fusion | flops 807403520 | bytes 8415232 | tf_op jit(solution)/shard_map/tm,atvb->amvb/dot_general | solution.py:56
  42.1 2.4 %copy.33 = f32[4,64,32,128]{3,2,1,0:T(8,128)S(1)} copy(f32[4,64,32,128]{3,1,2,0:T(8,128)S(1)} %fusion.11) | data formatting | bytes 8388608 | tf_op jit(solution)/shard_map/tm,atvb->amvb/transpose | solution.py:56
  44.5 0.6 slice_bitcast_fusion.1
  45.1 1.5 %fusion.19 = f32[5,16,128,16]{2,3,1,0:T(8,128)S(1)} fusion(f32[4,16,64,128]{3,2,1,0:T(8,128)S(1)} %get-tuple-element.15, f32[4,16,64,128]{3,2,1,0:T(8,128)S(1)} %get-tuple-element.14, f32[32,32]{1,0:T(8,128)S(1)} %get-tuple-element.24, f32[32,32]{1,0:T(8,128)S(1)} %get-tuple-element.25), kind=kOutput, calls=%fused_computation.19 | convolution fusion | flops 126485504 | bytes 4857856 | tf_op jit(solution)/shard_map/akpb,lp->akbl/dot_general | solution.py:61
  46.6 1.5 %fusion.18 = f32[5,16,128,16]{2,3,1,0:T(8,128)S(1)} fusion(f32[16,64,1,1]{1,0,3,2:T(8,128)S(1)} %fusion.25, f32[4,16,64,128]{3,2,1,0:T(8,128)S(1)} %get-tuple-element.15, f32[4,16,64,128]{3,2,1,0:T(8,128)S(1)} %get-tuple-element.14), kind=kOutput, calls=%fused_computation.18 | convolution fusion | flops 126484480 | bytes 4853760 | tf_op jit(solution)/shard_map/akpb,lp->akbl/dot_general | solution.py:62
  48.1 0.2 pad_add_fusion.4
  48.4 0.4 copy.36
  48.7 1.0 slice.74
  49.7 5.1 %collective-permute-start.2 = (f32[16,2064]{1,0:T(8,128)}, f32[16,2064]{1,0:T(8,128)}, u32[]{:S(2)}, u32[]{:S(2)}) collective-permute-start(f32[16,2064]{1,0:T(8,128)} %slice.74), channel_id=1, source_target_pairs={{0,8},{8,16},{16,24},{1,9},{9,17},{17,25},{2,10},{10,18},{18,26},{... | collective-permute-start | bytes 396296 | tf_op jit(solution)/shard_map/ppermute | solution.py:13
  54.8 0.4 copy.35
  55.1 0.3 slice.72
  55.5 1.2 pad_add_fusion.3
  56.6 2.1 %copy.37 = f32[3,16,129,16]{3,2,1,0:T(8,128)S(1)} copy(f32[3,16,129,16]{2,3,1,0:T(8,128)} %pad_add_fusion.3) | data formatting | bytes 792576 | tf_op jit(solution)/shard_map/slice | solution.py:79
  58.7 1.6 %slice.76 = f32[48,2064]{1,0:T(8,128)} reshape(f32[3,16,129,16]{3,2,1,0:T(8,128)S(1)} %copy.37) | data formatting | bytes 792576 | tf_op jit(solution)/shard_map/slice | solution.py:79
  60.3 0.0 collective-permute-done.2
  60.3 1.0 add.66
  61.4 0.7 pad_maximum_fusion.1
  62.1 2.1 %collective-permute-start.3 = (f32[64,16]{1,0:T(8,128)S(1)}, f32[64,16]{1,0:T(8,128)S(1)}, u32[]{:S(2)}, u32[]{:S(2)}) collective-permute-start(f32[64,16]{1,0:T(8,128)S(1)} %pad_maximum_fusion.1), channel_id=1, source_target_pairs={{0,1},{1,2},{2,3},{3,4},{4,5},{5,6},{6,7},{8,9},{9,10},{10,11},{11... | collective-permute-start | bytes 12296 | tf_op jit(solution)/shard_map/ppermute | solution.py:13
  64.2 0.8 collective-permute-done.3
  65.0 0.7 maximum_add_fusion
  65.8 2.1 %multiply_reduce_fusion = (f32[]{:T(128)}, f32[]{:T(128)}, f32[]{:T(128)}, f32[]{:T(128)}, f32[64,2048]{1,0:T(8,128)S(1)}) fusion(f32[64,2048]{1,0:T(8,128)} %param.6, f32[64,2048]{1,0:T(8,128)} %param.7, f32[48,2064]{1,0:T(8,128)} %slice.76, f32[16,2064]{1,0:T(8,128)S(1)} %add.66, f32[64,16]{1,0:T(8,128)S(1)} %maximum_add_fusion), kind=kLoop, calls=%fused_computation.27 | loop fusion | flops 1966076 | bytes 2105360 | tf_op jit(solution)/shard_map/reduce_sum | solution.py:90
  67.9 43.1 %all-reduce.4 = (f32[]{:T(128)}, f32[]{:T(128)}, f32[]{:T(128)}, f32[]{:T(128)}) all-reduce(f32[]{:T(128)} %get-tuple-element.5, f32[]{:T(128)} %get-tuple-element.6, f32[]{:T(128)} %get-tuple-element.4, f32[]{:T(128)} %get-tuple-element.3), channel_id=1, replica_groups=mesh['row'=4,'col'=8] {'row','col'}, use_global_device_ids=true, to_apply=%region_1.2 | all-reduce | flops 4 | bytes 32 | tf_op jit(solution)/shard_map/psum | solution.py:85
  114.9 0.0 copy-done.1
  114.9 0.0 copy-done.2
  114.9 0.0 copy-done.3
  114.9 1.2 %multiply_add_fusion = (f32[64,2048]{1,0:T(8,128)}, f32[64,2048]{1,0:T(8,128)}, f32[64,2048]{1,0:T(8,128)}) fusion(f32[64,2048]{1,0:T(8,128)S(1)} %copy-done.1, f32[]{:T(128)S(6)} %div.69, f32[64,2048]{1,0:T(8,128)S(1)} %copy-done.2, f32[64,2048]{1,0:T(8,128)S(1)} %get-tuple-element.13, f32[]{:T(128)S(6)} %div.68, f32[64,2048]{1,0:T(8,128)S(1)} %copy-done.3), kind=kLoop, calls=%fused_computation.26 | loop fusion | flops 786432 | bytes 3670024 | tf_op jit(solution)/shard_map/add | solution.py:98
  (10 shorter events, 0.1 us)
Async XLA Ops:
  1.4 3.4 %collective-permute-start = (f32[64,16]{1,0:T(8,128)S(1)}, f32[64,16]{1,0:T(8,128)S(1)}, u32[]{:S(2)}, u32[]{:S(2)}) collective-permute-start(f32[64,16]{1,0:T(8,128)S(1)} %slice.62), channel_id=1, source_target_pairs={{1,0},{2,1},{3,2},{4,3},{5,4},{6,5},{7,6},{9,8},{10,9},{11,10},{12... | collective-permute-start | bytes 12296 | tf_op jit(solution)/shard_map/ppermute | solution.py:13
  4.9 8.3 %collective-permute-start.1 = (f32[16,2064]{1,0:T(8,128)S(1)}, f32[16,2064]{1,0:T(8,128)S(1)}, u32[]{:S(2)}, u32[]{:S(2)}) collective-permute-start(f32[16,2064]{1,0:T(8,128)S(1)} %slice.82), channel_id=1, source_target_pairs={{8,0},{16,8},{24,16},{9,1},{17,9},{25,17},{10,2},{18,10},{26,18},{... | collective-permute-start | bytes 396296 | tf_op jit(solution)/shard_map/ppermute | solution.py:13
  16.5 8.1 %copy-start = (f32[5,16,129,16]{3,2,1,0:T(8,128)S(1)}, f32[5,16,129,16]{3,2,1,0:T(8,128)}, u32[]{:S(2)}) copy-start(f32[5,16,129,16]{3,2,1,0:T(8,128)} %reshape.132) | copy-start | bytes 1981444
  33.5 4.2 %copy-start.4 = (f32[4,128]{1,0:T(4,128)S(1)}, f32[4,128]{1,0:T(4,128)}, u32[]{:S(2)}) copy-start(f32[4,128]{1,0:T(4,128)} %param.8) | copy-start | bytes 6148
  49.7 10.6 %collective-permute-start.2 = (f32[16,2064]{1,0:T(8,128)}, f32[16,2064]{1,0:T(8,128)}, u32[]{:S(2)}, u32[]{:S(2)}) collective-permute-start(f32[16,2064]{1,0:T(8,128)} %slice.74), channel_id=1, source_target_pairs={{0,8},{8,16},{16,24},{1,9},{9,17},{17,25},{2,10},{10,18},{18,26},{... | collective-permute-start | bytes 396296 | tf_op jit(solution)/shard_map/ppermute | solution.py:13
  60.3 54.5 %copy-start.1 = (f32[64,2048]{1,0:T(8,128)S(1)}, f32[64,2048]{1,0:T(8,128)}, u32[]{:S(2)}) copy-start(f32[64,2048]{1,0:T(8,128)} %param.7) | copy-start | bytes 1572868
  60.3 54.5 %copy-start.2 = (f32[64,2048]{1,0:T(8,128)S(1)}, f32[64,2048]{1,0:T(8,128)}, u32[]{:S(2)}) copy-start(f32[64,2048]{1,0:T(8,128)} %param.6) | copy-start | bytes 1572868
  60.3 54.5 %copy-start.3 = (f32[64,2048]{1,0:T(8,128)S(1)}, f32[64,2048]{1,0:T(8,128)}, u32[]{:S(2)}) copy-start(f32[64,2048]{1,0:T(8,128)} %param.5) | copy-start | bytes 1572868
  62.1 2.9 %collective-permute-start.3 = (f32[64,16]{1,0:T(8,128)S(1)}, f32[64,16]{1,0:T(8,128)S(1)}, u32[]{:S(2)}, u32[]{:S(2)}) collective-permute-start(f32[64,16]{1,0:T(8,128)S(1)} %pad_maximum_fusion.1), channel_id=1, source_target_pairs={{0,1},{1,2},{2,3},{3,4},{4,5},{5,6},{6,7},{8,9},{9,10},{10,11},{11... | collective-permute-start | bytes 12296 | tf_op jit(solution)/shard_map/ppermute | solution.py:13
where the time goes:
time: 117 us; the launch traced here: 116 us
  blocking collectives  43.1 us (37%)
  matrix products  25.5 us (22%)
  local copies, waits for them, and re-layouts  17 us (15%)
  starting transfers between devices  9.7 us (8%)
  other arithmetic  8.51 us (7%)
  waiting for transfers between devices  7.62 us (7%)
  between operations  4.72 us (4%)
    psum x1, blocking collectives, per_device(): lax.psum((jnp.sum(residual * residual), jnp.sum(direction * applied), jnp...  43.1 us
    ppermute x4, starting transfers between devices, passed_along(): lax.ppermute(value, axis, [(source, source + steps) for source in range(l...  9.7 us
    dot_general x1, matrix products, analyze(): jnp.einsum('akbl,lp->akpb', blocks[:, :, 1:], column_table[16:], precisio...  8.09 us
    ppermute x4, waiting for transfers between devices, passed_along(): lax.ppermute(value, axis, [(source, source + steps) for source in range(l...  7.62 us
    dot_general x1, matrix products, analyze(): jnp.einsum('akbl,lp->akpb', blocks[:, :, :win_cols], column_table[:16], p...  5.8 us
    dot_general x1, matrix products, synthesize(): jnp.einsum('tm,atvb->amvb', row_table, coefficients, precision=precise)  4.37 us
    dot_general x1, matrix products, analyze(): return jnp.einsum('tm,amvb->atvb', row_table, paired, precision=precise)  4.16 us
    slice x2, local copies, waits for them, and re-layouts, per_device(): spread[16:height]  3.69 us
  transfers between devices with their start and end apart: 4, of which 2 were waited for; matrix products, arithmetic and copies ran while one was open for 7% of the time, Pallas kernels for 0%

commit v1 on v0

v1 whole, which is shorter than its diff:
```python
import functools

import jax
import jax.numpy as jnp
import ml_dtypes
import numpy as np
from jax import lax
from jax.experimental import pallas as pl
from jax.experimental.pallas import tpu as pltpu
from jax.sharding import PartitionSpec as P

MESH = pl.DeviceIdType.MESH
damping = 0.5


def split_host(table):
    table = np.asarray(table, np.float32)
    high = table.astype(ml_dtypes.bfloat16)
    low = (table - high.astype(np.float32)).astype(ml_dtypes.bfloat16)
    return jnp.asarray(high), jnp.asarray(low)


def host_tables(win_rows):
    j = np.arange(32)
    window = np.exp(-0.5 * ((j - 15.5) / 8.0) ** 2)
    basis = np.zeros((2, 16, 32))
    for w in range(16):
        phase = 2.0 * np.pi * w * j / 32.0
        basis[0, w] = np.sqrt(2.0) * np.cos(phase) if w else 1.0
        basis[1, w] = np.sqrt(2.0) * np.sin(phase) if w else (-1.0) ** j
    basis = basis * window / np.sqrt(32.0)
    col = np.zeros((256, 2, 16, 8))
    for b in range(8):
        col[112 + 16 * b : 144 + 16 * b, :, :, b] = basis.transpose(2, 0, 1)
    col = col.reshape(256, 256)
    height = 16 * win_rows
    row = np.zeros((32 * (win_rows + 1), height + 32))
    for a in range(win_rows + 1):
        row[32 * a : 32 * a + 32, 16 * a : 16 * a + 32] = basis.reshape(32, 32)
    row_back = row.T[16 : 16 + height]
    even = np.zeros((2, 16, 32))
    odd = np.zeros((2, 16, 32))
    for h in range(2):
        for w in range(16):
            f = 16 if (h == 1 and w == 0) else w
            even[h, w, f] += 0.5
            even[h, w, -f % 32] += 0.5
            sign = 1.0 - 2.0 * h
            odd[h, w, f] += 0.5 * sign
            odd[h, w, -f % 32] -= 0.5 * sign
    even, odd = even.reshape(32, 32), odd.reshape(32, 32)
    left = np.stack([even, -odd]).astype(np.float32)
    right = np.stack([np.repeat(even.T, 8, axis=1), np.repeat(odd.T, 8, axis=1)]).astype(np.float32)
    return split_host(col), split_host(row), split_host(row_back), jnp.asarray(left), jnp.asarray(right)


def split(value):
    high = value.astype(jnp.bfloat16)
    low = (value - high.astype(jnp.float32)).astype(jnp.bfloat16)
    return high, low


def dot3(a, b, dims=((1,), (0,))):
    def dot(x, y):
        return lax.dot_general(x, y, (dims, ((), ())), preferred_element_type=jnp.float32)

    return dot(a[0], b[0]) + (dot(a[0], b[1]) + dot(a[1], b[0]))


def kernel(
    n_row,
    n_col,
    direction,
    residual,
    weight,
    freq,
    col_h,
    col_l,
    row_h,
    row_l,
    back_h,
    back_l,
    left,
    right,
    applied_out,
    scalars,
    ext,
    res,
    acc,
    own_w,
    got_w,
    spread_w,
    mix,
    red_col,
    red_row,
    part,
    local_sem,
    halo_send,
    halo_recv,
    w_send,
    w_recv,
    col_send,
    col_recv,
    row_send,
    row_recv,
):
    r = lax.axis_index("row")
    c = lax.axis_index("col")
    height, breadth = direction.shape
    win_rows = height // 16
    chunks = breadth // 128 + 1

    fetch_own = pltpu.make_async_copy(direction, ext.at[16 : 16 + height, 128 : 128 + breadth], local_sem.at[0])
    fetch_own.start()
    fetch_res = pltpu.make_async_copy(residual, res, local_sem.at[1])
    fetch_res.start()

    def exists(dr, dc):
        ok = jnp.bool_(True)
        if dr == 1:
            ok = r < n_row - 1
        if dr == -1:
            ok = r > 0
        if dc == 1:
            ok = jnp.logical_and(ok, c < n_col - 1)
        if dc == -1:
            ok = jnp.logical_and(ok, c > 0)
        return ok

    around = [(dr, dc) for dr in (0, -1, 1) for dc in (0, -1, 1) if (dr, dc) != (0, 0)]

    barrier = pltpu.get_barrier_semaphore()
    for k in range(1, n_col):
        pl.semaphore_signal(barrier, inc=1, device_id=(r, lax.rem(c + k, n_col)), device_id_type=MESH)
    for k in range(1, n_row):
        pl.semaphore_signal(barrier, inc=1, device_id=(lax.rem(r + k, n_row), c), device_id_type=MESH)
    for dr, dc in around:
        if dr != 0 and dc != 0:

            @pl.when(exists(dr, dc))
            def _(dr=dr, dc=dc):
                pl.semaphore_signal(barrier, inc=1, device_id=(r + dr, c + dc), device_id_type=MESH)

    vertical = jnp.where(r > 0, 1, 0) + jnp.where(r < n_row - 1, 1, 0)
    horizontal = jnp.where(c > 0, 1, 0) + jnp.where(c < n_col - 1, 1, 0)

    own_w[...] = jnp.zeros_like(own_w)
    own_w[0:win_rows, :] = weight[...]

    pl.semaphore_wait(barrier, n_col - 1 + n_row - 1 + vertical * horizontal)

    src_rows = {0: slice(0, height), -1: slice(0, 16), 1: slice(height - 16, height)}
    src_cols = {0: slice(0, breadth), -1: slice(0, 128), 1: slice(breadth - 128, breadth)}
    dst_rows = {0: slice(16, 16 + height), -1: slice(16 + height, 32 + height), 1: slice(0, 16)}
    dst_cols = {0: slice(128, 128 + breadth), -1: slice(128 + breadth, 256 + breadth), 1: slice(0, 128)}

    def halo(i):
        dr, dc = around[i]
        return pltpu.make_async_remote_copy(
            src_ref=direction.at[src_rows[dr], src_cols[dc]],
            dst_ref=ext.at[dst_rows[dr], dst_cols[dc]],
            send_sem=halo_send.at[i],
            recv_sem=halo_recv.at[i],
            device_id=(r + dr, c + dc),
            device_id_type=MESH,
        )

    forward = [(0, 1), (1, 0), (1, 1)]

    def weights(i):
        dr, dc = forward[i]
        return pltpu.make_async_remote_copy(
            src_ref=own_w,
            dst_ref=got_w.at[i],
            send_sem=w_send.at[i],
            recv_sem=w_recv.at[i],
            device_id=(r + dr, c + dc),
            device_id_type=MESH,
        )

    order = sorted(range(8), key=lambda i: around[i][1] != 0)
    for i in order:

        @pl.when(exists(*around[i]))
        def _(i=i):
            halo(i).start()

    for i in range(3):

        @pl.when(exists(*forward[i]))
        def _(i=i):
            weights(i).start()

    for i, (dr, dc) in enumerate(around):

        @pl.when(jnp.logical_not(exists(-dr, -dc)))
        def _(dr=dr, dc=dc):
            rows, cols = dst_rows[dr], dst_cols[dc]
            ext[rows, cols] = jnp.zeros((rows.stop - rows.start, cols.stop - cols.start), jnp.float32)

    for i, (dr, dc) in enumerate(forward):

        @pl.when(jnp.logical_not(exists(-dr, -dc)))
        def _(i=i):
            got_w[i] = jnp.zeros_like(own_w)

    for m in range(2):
        folded = jnp.dot(left[m], freq[...], precision=lax.Precision.HIGHEST, preferred_element_type=jnp.float32)
        mix[m] = jnp.dot(folded, right[m], precision=lax.Precision.HIGHEST, preferred_element_type=jnp.float32)

    acc[...] = jnp.zeros_like(acc)
    fetch_res.wait()
    fetch_own.wait()

    for i in range(3):
        dr, dc = forward[i]

        @pl.when(exists(-dr, -dc))
        def _(i=i):
            weights(i).wait_recv()

    lane = lax.broadcasted_iota(jnp.int32, (8, 128), 1)
    sub = lax.broadcasted_iota(jnp.int32, (8, 128), 0)

    def stacked(above, here):
        return jnp.where(sub == 0, pltpu.roll(above, 8 - (win_rows - 1), 0), pltpu.roll(here, 1, 0))

    main_w = pltpu.roll(stacked(got_w[1], own_w[...]), 1, 1)
    left_w = pltpu.roll(stacked(got_w[2], got_w[0]), 1, 1)
    shifted = jnp.where(lane == 0, left_w, main_w)
    for k in range(chunks):
        if k == chunks - 1:
            x = jnp.where(lane == 0, main_w, 0.0)
        else:
            x = jnp.where(lane < 8, pltpu.roll(shifted, (128 - 8 * k) % 128, 1) if k else shifted, 0.0)
        for step in (8, 16, 32, 64):
            x = x + pltpu.roll(x, step, 1)
        spread_w[k] = x

    for i in range(8):
        dr, dc = around[i]

        @pl.when(exists(-dr, -dc))
        def _(i=i):
            halo(i).wait_recv()

    even = mix[0]
    odd = mix[1]

    def one_chunk(k):
        start = k * 128 if isinstance(k, int) else pl.multiple_of(k * 128, 128)
        lanes = pl.ds(start, 256)
        col = (col_h[...], col_l[...])
        first = dot3(split(ext[:, lanes]), col)
        coef = dot3((row_h[...], row_l[...]), split(first))
        pieces = []
        for a in range(win_rows + 1):
            z = coef[32 * a : 32 * a + 32]
            swapped = jnp.concatenate([z[16:], z[:16]], axis=0)
            swapped = jnp.concatenate([swapped[:, 128:], swapped[:, :128]], axis=1)
            w = spread_w[k, a : a + 1, :]
            pieces.append((even * z + odd * swapped) * jnp.concatenate([w, w], axis=1))
        weighted = jnp.concatenate(pieces, axis=0)
        rows = dot3((back_h[...], back_l[...]), split(weighted))
        acc[:, lanes] += dot3(split(rows), col, ((1,), (1,)))

    group = 4
    whole_groups = (chunks - 1) // group

    def body(g, carry):
        for k in range(group):
            one_chunk(g * group + k)
        return carry

    lax.fori_loop(0, whole_groups, body, 0)
    for k in range(whole_groups * group, chunks):
        one_chunk(k)

    def sums(k, carry):
        lanes = pl.ds(pl.multiple_of(k * 128, 128), 128)
        inner = pl.ds(pl.multiple_of(k * 128 + 128, 128), 128)
        d = ext[16 : 16 + height, inner]
        e = res[:, lanes]
        q = acc[:, inner] + damping * d
        acc[:, inner] = q
        terms = (e * e, d * q, e * q, q * q)
        return tuple(t + jnp.sum(v.reshape(-1, 8, 128), axis=0) for t, v in zip(carry, terms))

    zero = jnp.zeros((8, 128), jnp.float32)
    totals = lax.fori_loop(0, breadth // 128, sums, (zero,) * 4)
    store = pltpu.make_async_copy(acc.at[:, 128 : 128 + breadth], applied_out, local_sem.at[2])
    store.start()

    tile = jnp.zeros((8, 128), jnp.float32)
    for i, t in enumerate(totals):
        tile = jnp.where(sub == i, jnp.sum(t, axis=0, keepdims=True), tile)

    def exchange(n, me, target, slots, sends, recvs):
        for k in range(1, n):
            to = lax.rem(me + k, n)
            pltpu.make_async_remote_copy(
                src_ref=part,
                dst_ref=slots.at[me],
                send_sem=sends.at[k - 1],
                recv_sem=recvs.at[me],
                device_id=target(to),
                device_id_type=MESH,
            ).start()
        slots[me] = part[...]
        for k in range(1, n):
            source = lax.rem(me + k, n)
            pltpu.make_async_remote_copy(
                src_ref=part,
                dst_ref=slots.at[source],
                send_sem=sends.at[k - 1],
                recv_sem=recvs.at[source],
                device_id=target(source),
                device_id_type=MESH,
            ).wait()
        total = slots[0]
        for k in range(1, n):
            total = total + slots[k]
        return total

    part[...] = tile
    tile = exchange(n_col, c, lambda to: (r, to), red_col, col_send, col_recv)
    part[...] = tile
    tile = exchange(n_row, r, lambda to: (to, c), red_row, row_send, row_recv)

    total = jnp.sum(tile, axis=1, keepdims=True)
    norm_now, curvature, cross, image = (jnp.broadcast_to(total[i : i + 1], (1, 128)) for i in range(4))
    step_length = norm_now / curvature
    norm_next = norm_now - 2.0 * step_length * cross + step_length * step_length * image
    scalars[0:1, :] = step_length
    scalars[1:2, :] = norm_next / norm_now
    scalars[2:8, :] = jnp.zeros((6, 128), jnp.float32)

    for i in range(8):

        @pl.when(exists(*around[i]))
        def _(i=i):
            halo(i).wait_send()

    for i in range(3):

        @pl.when(exists(*forward[i]))
        def _(i=i):
            weights(i).wait_send()

    store.wait()


def per_device(n_row, n_col, iterate, residual, direction, window_weight, freq_weight):
    height, breadth = direction.shape
    win_rows = height // 16
    col, row, back, left, right = host_tables(win_rows)
    vmem = pl.BlockSpec(memory_space=pltpu.VMEM)
    hbm = pl.BlockSpec(memory_space=pl.ANY)
    dma = pltpu.SemaphoreType.DMA
    f32 = jnp.float32
    applied, scalars = pl.pallas_call(
        functools.partial(kernel, n_row, n_col),
        out_shape=(jax.ShapeDtypeStruct((height, breadth), f32), jax.ShapeDtypeStruct((8, 128), f32)),
        in_specs=[hbm, hbm] + [vmem] * 10,
        out_specs=(hbm, vmem),
        scratch_shapes=[
            pltpu.VMEM((height + 32, breadth + 256), f32),
            pltpu.VMEM((height, breadth), f32),
            pltpu.VMEM((height, breadth + 256), f32),
            pltpu.VMEM((8, 128), f32),
            pltpu.VMEM((3, 8, 128), f32),
            pltpu.VMEM((breadth // 128 + 1, 8, 128), f32),
            pltpu.VMEM((2, 32, 256), f32),
            pltpu.VMEM((n_col, 8, 128), f32),
            pltpu.VMEM((n_row, 8, 128), f32),
            pltpu.VMEM((8, 128), f32),
            dma((3,)),
            dma((8,)),
            dma((8,)),
            dma((3,)),
            dma((3,)),
            dma((n_col,)),
            dma((n_col,)),
            dma((n_row,)),
            dma((n_row,)),
        ],
        compiler_params=pltpu.CompilerParams(
            collective_id=0, has_side_effects=True, vmem_limit_bytes=32 * 1024 * 1024
        ),
        cost_estimate=pl.CostEstimate(flops=5_000_000_000, bytes_accessed=2_000_000, transcendentals=0),
    )(direction, residual, window_weight, freq_weight, *col, *row, *back, left, right)
    step_length = scalars[0:1, 0:1]
    ratio = scalars[1:2, 0:1]
    new_iterate = iterate + step_length * direction
    new_residual = residual - step_length * applied
    new_direction = new_residual + ratio * direction
    return (new_iterate, new_residual, new_direction)


def solution(mesh):
    return jax.shard_map(
        functools.partial(per_device, mesh.shape["row"], mesh.shape["col"]),
        mesh=mesh,
        in_specs=(P("row", "col"), P("row", "col"), P("row", "col"), P("row", "col"), P()),
        out_specs=(P("row", "col"), P("row", "col"), P("row", "col")),
        check_vma=False,
    )
```

time: 117 us -> 44.5 us (0.38)
  blocking collectives: 43.1 us -> 0 us
  Pallas kernels: 0 us -> 30.1 us
  matrix products: 25.5 us -> 0 us
  starting transfers between devices: 9.7 us -> 0 us
  waiting for transfers between devices: 7.62 us -> 0 us
  local copies, waits for them, and re-layouts: 17 us -> 10.5 us
  other arithmetic: 8.51 us -> 2.52 us
  between operations: 4.72 us -> 0.66 us
    psum x1 -> x0, blocking collectives: 43.1 us -> none  [per_device(): lax.psum((jnp.sum(residual * residual), jnp.sum(direction * applied), jnp...]
    pallas_call x0 -> x1, Pallas kernels: none -> 30.1 us  [per_device(): pl.pallas_call(functools.partial(kernel, n_row, n_col), out_shape=(jax.Sh...]
    dot_general x6 -> x0, matrix products: 25.5 us -> none  [the longest x1 8.09 us: analyze(): jnp.einsum('akbl,lp->akpb', blocks[:, :, 1:], column_table[16:], precisio...]
    ppermute x4 -> x0, starting transfers between devices: 9.7 us -> none  [passed_along(): lax.ppermute(value, axis, [(source, source + steps) for source in range(l...]
    unnamed x11 -> x26, local copies, waits for them, and re-layouts: 1.1 us -> 9.95 us
    ppermute x4 -> x0, waiting for transfers between devices: 7.62 us -> none  [passed_along(): lax.ppermute(value, axis, [(source, source + steps) for source in range(l...]
    slice x9 -> x1, local copies, waits for them, and re-layouts: 7.12 us -> 0.58 us  [per_device(): ratio = scalars[1:2, 0:1]]
    reshape x1 -> x0, local copies, waits for them, and re-layouts: 3.26 us -> none  [analyze(): blocks = region.reshape(win_rows + 1, 16, win_cols + 1, 16)]
  transfers between devices with their start and end apart: 4 -> 0, of which waited for: 2 -> 0; matrix products, arithmetic and copies ran while one was open for 7% -> 0% of each run, Pallas kernels for 0% -> 0%
where the time goes in v1:
time: 44.5 us; the launch traced here: 43.8 us
  Pallas kernels  30.1 us (68%)
  local copies, waits for them, and re-layouts  10.5 us (24%)
  other arithmetic  2.52 us (6%)
  between operations  0.66 us (1%)
    pallas_call x1, Pallas kernels, per_device(): pl.pallas_call(functools.partial(kernel, n_row, n_col), out_shape=(jax.Sh...  30.1 us
    unnamed x26, local copies, waits for them, and re-layouts  9.95 us
    add x1, other arithmetic, per_device(): new_direction = new_residual + ratio * direction  2.52 us

profile of v1, /device:TPU:0, one launch (start us, length us, event | category | flops | bytes accessed | tf_op | source)
XLA Modules:
  0.0 43.8 jit_solution(5446377133835059036)
XLA Ops:
  0.6 0.0 copy-start
  0.6 1.0 %copy-done = f32[64,2048]{1,0:T(8,128)S(1)} copy-done((f32[64,2048]{1,0:T(8,128)S(1)}, f32[64,2048]{1,0:T(8,128)}, u32[]{:S(2)}) %copy-start) | copy-done | bytes 524312
  1.7 0.0 copy-start.1
  1.7 1.0 %copy-done.1 = f32[64,2048]{1,0:T(8,128)S(1)} copy-done((f32[64,2048]{1,0:T(8,128)S(1)}, f32[64,2048]{1,0:T(8,128)}, u32[]{:S(2)}) %copy-start.1) | copy-done | bytes 524312
  2.7 0.0 copy-start.2
  2.7 0.7 %copy-done.2 = f32[32,32]{1,0:T(8,128)S(1)} copy-done((f32[32,32]{1,0:T(8,128)S(1)}, f32[32,32]{1,0:T(8,128)}, u32[]{:S(2)}) %copy-start.2) | copy-done | bytes 4120
  3.4 0.0 copy-start.3
  3.4 0.7 %copy-done.3 = f32[4,128]{1,0:T(4,128)S(1)} copy-done((f32[4,128]{1,0:T(4,128)S(1)}, f32[4,128]{1,0:T(4,128)}, u32[]{:S(2)}) %copy-start.3) | copy-done | bytes 2072
  4.1 0.0 copy-start.4
  4.1 0.9 %copy-done.4 = bf16[256,256]{1,0:T(8,128)(2,1)S(1)} copy-done((bf16[256,256]{1,0:T(8,128)(2,1)S(1)}, bf16[256,256]{1,0:T(8,128)(2,1)}, u32[]{:S(2)}) %copy-start.4) | copy-done | bytes 131096
  5.0 0.0 copy-start.5
  5.0 0.9 %copy-done.5 = bf16[256,256]{1,0:T(8,128)(2,1)S(1)} copy-done((bf16[256,256]{1,0:T(8,128)(2,1)S(1)}, bf16[256,256]{1,0:T(8,128)(2,1)}, u32[]{:S(2)}) %copy-start.5) | copy-done | bytes 131096
  5.9 0.0 copy-start.6
  5.9 0.8 %copy-done.6 = f32[2,32,256]{2,1,0:T(8,128)S(1)} copy-done((f32[2,32,256]{2,1,0:T(8,128)S(1)}, f32[2,32,256]{2,1,0:T(8,128)}, u32[]{:S(2)}) %copy-start.6) | copy-done | bytes 65560
  6.8 0.0 copy-start.7
  6.8 0.8 %copy-done.7 = bf16[160,96]{1,0:T(8,128)(2,1)S(1)} copy-done((bf16[160,96]{1,0:T(8,128)(2,1)S(1)}, bf16[160,96]{1,0:T(8,128)(2,1)}, u32[]{:S(2)}) %copy-start.7) | copy-done | bytes 30744
  7.5 0.0 copy-start.8
  7.5 0.8 %copy-done.8 = bf16[160,96]{1,0:T(8,128)(2,1)S(1)} copy-done((bf16[160,96]{1,0:T(8,128)(2,1)S(1)}, bf16[160,96]{1,0:T(8,128)(2,1)}, u32[]{:S(2)}) %copy-start.8) | copy-done | bytes 30744
  8.3 0.0 copy-start.9
  8.3 0.8 %copy-done.9 = f32[2,32,32]{2,1,0:T(8,128)S(1)} copy-done((f32[2,32,32]{2,1,0:T(8,128)S(1)}, f32[2,32,32]{2,1,0:T(8,128)}, u32[]{:S(2)}) %copy-start.9) | copy-done | bytes 8216
  9.1 0.0 copy-start.10
  9.1 0.8 %copy-done.10 = bf16[64,160]{1,0:T(8,128)(2,1)S(1)} copy-done((bf16[64,160]{1,0:T(8,128)(2,1)S(1)}, bf16[64,160]{1,0:T(8,128)(2,1)}, u32[]{:S(2)}) %copy-start.10) | copy-done | bytes 20504
  9.8 0.0 copy-start.11
  9.8 0.8 %copy-done.11 = bf16[64,160]{1,0:T(8,128)(2,1)S(1)} copy-done((bf16[64,160]{1,0:T(8,128)(2,1)S(1)}, bf16[64,160]{1,0:T(8,128)(2,1)}, u32[]{:S(2)}) %copy-start.11) | copy-done | bytes 20504
  10.6 0.0 copy-start.12
  10.6 30.1 %shard_map.148 = (f32[64,2048]{1,0:T(8,128)S(1)}, f32[8,128]{1,0:T(8,128)S(1)}) custom-call(f32[64,2048]{1,0:T(8,128)S(1)} %copy-done, f32[64,2048]{1,0:T(8,128)S(1)} %copy-done.1, f32[4,128]{1,0:T(4,128)S(1)} %copy-done.3, f32[32,32]{1,0:T(8,128)S(1)} %copy-done.2, bf16[256,256]{1,0:T(8,128)(2,1)S(1)} %copy-done.5, bf16[256,256]{1,0:T(8,128)(2,1)S(1)} %copy-done.4, ...), custom_call_target="tpu_custom_call" | custom-call | flops 5000000000 | bytes 2000000 | tf_op jit(solution)/shard_map/pallas_call | solution.py:361
  40.7 0.6 %fusion = (f32[1,1]{1,0:T(1,128)}, f32[1,1]{1,0:T(1,128)}) fusion(f32[8,128]{1,0:T(8,128)S(1)} %get-tuple-element.5), kind=kLoop, calls=%fused_computation.3 | loop fusion | bytes 16 | tf_op jit(solution)/shard_map/slice | solution.py:393
  41.3 0.0 copy-done.12
  41.3 2.5 %multiply_add_fusion = (f32[64,2048]{1,0:T(8,128)}, f32[64,2048]{1,0:T(8,128)}, f32[64,2048]{1,0:T(8,128)}) fusion(f32[64,2048]{1,0:T(8,128)S(1)} %copy-done, f32[]{:T(128)} %bitcast.1, f32[64,2048]{1,0:T(8,128)S(1)} %copy-done.1, f32[64,2048]{1,0:T(8,128)S(1)} %get-tuple-element.6, f32[]{:T(128)} %bitcast, f32[64,2048]{1,0:T(8,128)S(1)} %copy-done.12), kind=kLoop, calls=%fused_computation | loop fusion | flops 786432 | bytes 3670024 | tf_op jit(solution)/shard_map/add | solution.py:396
Async XLA Ops:
  0.6 1.0 %copy-start = (f32[64,2048]{1,0:T(8,128)S(1)}, f32[64,2048]{1,0:T(8,128)}, u32[]{:S(2)}) copy-start(f32[64,2048]{1,0:T(8,128)} %direction.1) | copy-start | bytes 1572868
  1.7 1.0 %copy-start.1 = (f32[64,2048]{1,0:T(8,128)S(1)}, f32[64,2048]{1,0:T(8,128)}, u32[]{:S(2)}) copy-start(f32[64,2048]{1,0:T(8,128)} %residual.1) | copy-start | bytes 1572868
  2.7 0.7 %copy-start.2 = (f32[32,32]{1,0:T(8,128)S(1)}, f32[32,32]{1,0:T(8,128)}, u32[]{:S(2)}) copy-start(f32[32,32]{1,0:T(8,128)} %freq.1) | copy-start | bytes 12292
  3.4 0.7 %copy-start.3 = (f32[4,128]{1,0:T(4,128)S(1)}, f32[4,128]{1,0:T(4,128)}, u32[]{:S(2)}) copy-start(f32[4,128]{1,0:T(4,128)} %weight.1) | copy-start | bytes 6148
  4.1 0.9 %copy-start.4 = (bf16[256,256]{1,0:T(8,128)(2,1)S(1)}, bf16[256,256]{1,0:T(8,128)(2,1)}, u32[]{:S(2)}) copy-start(bf16[256,256]{1,0:T(8,128)(2,1)} %constant.17.clone.col_l) | copy-start | bytes 393220
  5.0 0.9 %copy-start.5 = (bf16[256,256]{1,0:T(8,128)(2,1)S(1)}, bf16[256,256]{1,0:T(8,128)(2,1)}, u32[]{:S(2)}) copy-start(bf16[256,256]{1,0:T(8,128)(2,1)} %constant.16.clone.col_h) | copy-start | bytes 393220
  5.9 0.8 %copy-start.6 = (f32[2,32,256]{2,1,0:T(8,128)S(1)}, f32[2,32,256]{2,1,0:T(8,128)}, u32[]{:S(2)}) copy-start(f32[2,32,256]{2,1,0:T(8,128)} %constant.23.clone.right) | copy-start | bytes 196612
  6.8 0.8 %copy-start.7 = (bf16[160,96]{1,0:T(8,128)(2,1)S(1)}, bf16[160,96]{1,0:T(8,128)(2,1)}, u32[]{:S(2)}) copy-start(bf16[160,96]{1,0:T(8,128)(2,1)} %constant.19.clone.row_l) | copy-start | bytes 92164
  7.5 0.8 %copy-start.8 = (bf16[160,96]{1,0:T(8,128)(2,1)S(1)}, bf16[160,96]{1,0:T(8,128)(2,1)}, u32[]{:S(2)}) copy-start(bf16[160,96]{1,0:T(8,128)(2,1)} %constant.18.clone.row_h) | copy-start | bytes 92164
  8.3 0.8 %copy-start.9 = (f32[2,32,32]{2,1,0:T(8,128)S(1)}, f32[2,32,32]{2,1,0:T(8,128)}, u32[]{:S(2)}) copy-start(f32[2,32,32]{2,1,0:T(8,128)} %constant.22.clone.left) | copy-start | bytes 24580
  9.1 0.8 %copy-start.10 = (bf16[64,160]{1,0:T(8,128)(2,1)S(1)}, bf16[64,160]{1,0:T(8,128)(2,1)}, u32[]{:S(2)}) copy-start(bf16[64,160]{1,0:T(8,128)(2,1)} %constant.21.clone.back_l) | copy-start | bytes 61444
  9.8 0.8 %copy-start.11 = (bf16[64,160]{1,0:T(8,128)(2,1)S(1)}, bf16[64,160]{1,0:T(8,128)(2,1)}, u32[]{:S(2)}) copy-start(bf16[64,160]{1,0:T(8,128)(2,1)} %constant.20.clone.back_h) | copy-start | bytes 61444
  10.6 30.7 %copy-start.12 = (f32[64,2048]{1,0:T(8,128)S(1)}, f32[64,2048]{1,0:T(8,128)}, u32[]{:S(2)}) copy-start(f32[64,2048]{1,0:T(8,128)} %param.13) | copy-start | bytes 1572868

commit v2 on v1

--- a/solution.py
+++ b/solution.py
@@ -13,11 +13,11 @@
 damping = 0.5
 
 
-def split_host(table):
+def split_host(table, axis):
     table = np.asarray(table, np.float32)
     high = table.astype(ml_dtypes.bfloat16)
     low = (table - high.astype(np.float32)).astype(ml_dtypes.bfloat16)
-    return jnp.asarray(high), jnp.asarray(low)
+    return jnp.asarray(np.concatenate([high, high, low], axis=axis).astype(np.float32))
 
 
 def host_tables(win_rows):
@@ -51,7 +51,9 @@
     even, odd = even.reshape(32, 32), odd.reshape(32, 32)
     left = np.stack([even, -odd]).astype(np.float32)
     right = np.stack([np.repeat(even.T, 8, axis=1), np.repeat(odd.T, 8, axis=1)]).astype(np.float32)
-    return split_host(col), split_host(row), split_host(row_back), jnp.asarray(left), jnp.asarray(right)
+    tables = (jnp.asarray(col, jnp.float32), jnp.asarray(col.T, jnp.float32))
+    tables = tables + (split_host(row, 1), split_host(row_back, 1))
+    return tables + (jnp.asarray(left), jnp.asarray(right))
 
 
 def split(value):
@@ -60,11 +62,12 @@
     return high, low
 
 
-def dot3(a, b, dims=((1,), (0,))):
-    def dot(x, y):
-        return lax.dot_general(x, y, (dims, ((), ())), preferred_element_type=jnp.float32)
-
-    return dot(a[0], b[0]) + (dot(a[0], b[1]) + dot(a[1], b[0]))
+def thrice(high, low, axis):
+    return jnp.concatenate([high, low, high], axis=axis)
+
+
+def dot(x, y):
+    return jnp.dot(x, y, preferred_element_type=jnp.float32)
 
 
 def kernel(
@@ -72,21 +75,31 @@
     n_col,
     direction,
     residual,
+    weight_in,
+    freq_in,
+    col_in,
+    col_back_in,
+    row_in,
+    row_back_in,
+    left_in,
+    right_in,
+    applied_out,
+    scalars,
     weight,
     freq,
-    col_h,
-    col_l,
-    row_h,
-    row_l,
-    back_h,
-    back_l,
+    col,
+    col_back,
+    row,
+    row_back,
     left,
     right,
-    applied_out,
-    scalars,
+    col3,
+    col_back3,
     ext,
     res,
     acc,
+    first_h,
+    first_l,
     own_w,
     got_w,
     spread_w,
@@ -110,10 +123,19 @@
     win_rows = height // 16
     chunks = breadth // 128 + 1
 
-    fetch_own = pltpu.make_async_copy(direction, ext.at[16 : 16 + height, 128 : 128 + breadth], local_sem.at[0])
-    fetch_own.start()
-    fetch_res = pltpu.make_async_copy(residual, res, local_sem.at[1])
-    fetch_res.start()
+    places = (
+        (weight_in, weight),
+        (direction, ext.at[16 : 16 + height, 128 : 128 + breadth]),
+        (col_in, col),
+        (freq_in, freq),
+        (left_in, left),
+        (right_in, right),
+        (row_in, row),
+        (residual, res),
+        (row_back_in, row_back),
+        (col_back_in, col_back),
+    )
+    fetches = [pltpu.make_async_copy(a, b, local_sem.at[i]) for i, (a, b) in enumerate(places)]
 
     def exists(dr, dc):
         ok = jnp.bool_(True)
@@ -144,7 +166,11 @@
     vertical = jnp.where(r > 0, 1, 0) + jnp.where(r < n_row - 1, 1, 0)
     horizontal = jnp.where(c > 0, 1, 0) + jnp.where(c < n_col - 1, 1, 0)
 
+    for fetch in fetches:
+        fetch.start()
+
     own_w[...] = jnp.zeros_like(own_w)
+    fetches[0].wait()
     own_w[0:win_rows, :] = weight[...]
 
     pl.semaphore_wait(barrier, n_col - 1 + n_row - 1 + vertical * horizontal)
@@ -204,13 +230,48 @@
         def _(i=i):
             got_w[i] = jnp.zeros_like(own_w)
 
+    acc[...] = jnp.zeros_like(acc)
+    def stack_split(table, stack):
+        size = table.shape[0]
+        h, l = split(table[...])
+        stack[0:size, :] = h
+        stack[size : 2 * size, :] = h
+        stack[2 * size :, :] = l
+
+    fetches[2].wait()
+    stack_split(col, col3)
+    fetches[1].wait()
+
+    def columns(regions):
+        high, low = [], []
+        for k, top, end in regions:
+            start = k * 128 if isinstance(k, int) else pl.multiple_of(k * 128, 128)
+            h, l = split(ext[top:end, pl.ds(start, 256)])
+            high.append(h)
+            low.append(l)
+        high, low = jnp.concatenate(high, axis=0), jnp.concatenate(low, axis=0)
+        h, l = split(dot(thrice(high, low, 1), col3[...]))
+        at = 0
+        for k, top, end in regions:
+            first_h[k, top:end, :] = h[at : at + end - top]
+            first_l[k, top:end, :] = l[at : at + end - top]
+            at += end - top
+
+    inner = chunks - 2
+    group = 5 if inner % 5 == 0 else 1
+
+    def own_columns(g, carry):
+        columns([(1 + g * group + k, 16, 16 + height) for k in range(group)])
+        return carry
+
+    lax.fori_loop(0, inner // group, own_columns, 0)
+
+    for i in range(3, len(fetches)):
+        fetches[i].wait()
+    stack_split(col_back, col_back3)
     for m in range(2):
         folded = jnp.dot(left[m], freq[...], precision=lax.Precision.HIGHEST, preferred_element_type=jnp.float32)
         mix[m] = jnp.dot(folded, right[m], precision=lax.Precision.HIGHEST, preferred_element_type=jnp.float32)
-
-    acc[...] = jnp.zeros_like(acc)
-    fetch_res.wait()
-    fetch_own.wait()
 
     for i in range(3):
         dr, dc = forward[i]
@@ -247,12 +308,13 @@
     even = mix[0]
     odd = mix[1]
 
-    def one_chunk(k):
-        start = k * 128 if isinstance(k, int) else pl.multiple_of(k * 128, 128)
-        lanes = pl.ds(start, 256)
-        col = (col_h[...], col_l[...])
-        first = dot3(split(ext[:, lanes]), col)
-        coef = dot3((row_h[...], row_l[...]), split(first))
+    rim = [(0, 0, height + 32), (chunks - 1, 0, height + 32)]
+    for k in range(1, chunks - 1):
+        rim += [(k, 0, 16), (k, 16 + height, 32 + height)]
+    columns(rim)
+
+    def rows_of(k):
+        coef = dot(row[...].astype(jnp.bfloat16), thrice(first_h[k], first_l[k], 0))
         pieces = []
         for a in range(win_rows + 1):
             z = coef[32 * a : 32 * a + 32]
@@ -260,35 +322,39 @@
             swapped = jnp.concatenate([swapped[:, 128:], swapped[:, :128]], axis=1)
             w = spread_w[k, a : a + 1, :]
             pieces.append((even * z + odd * swapped) * jnp.concatenate([w, w], axis=1))
-        weighted = jnp.concatenate(pieces, axis=0)
-        rows = dot3((back_h[...], back_l[...]), split(weighted))
-        acc[:, lanes] += dot3(split(rows), col, ((1,), (1,)))
-
-    group = 4
-    whole_groups = (chunks - 1) // group
+        h, l = split(jnp.concatenate(pieces, axis=0))
+        return split(dot(row_back[...].astype(jnp.bfloat16), thrice(h, l, 0)))
+
+    def chunk_group(ks):
+        parts = [rows_of(k) for k in ks]
+        h = jnp.concatenate([p[0] for p in parts], axis=0)
+        l = jnp.concatenate([p[1] for p in parts], axis=0)
+        out = dot(thrice(h, l, 1), col_back3[...])
+        for i, k in enumerate(ks):
+            start = k * 128 if isinstance(k, int) else pl.multiple_of(k * 128, 128)
+            acc[:, pl.ds(start, 256)] += out[i * height : (i + 1) * height]
 
     def body(g, carry):
-        for k in range(group):
-            one_chunk(g * group + k)
+        chunk_group([g * group + k for k in range(group)])
         return carry
 
-    lax.fori_loop(0, whole_groups, body, 0)
-    for k in range(whole_groups * group, chunks):
-        one_chunk(k)
+    lax.fori_loop(0, chunks // group, body, 0)
+    if chunks % group:
+        chunk_group(list(range(chunks - chunks % group, chunks)))
 
     def sums(k, carry):
         lanes = pl.ds(pl.multiple_of(k * 128, 128), 128)
-        inner = pl.ds(pl.multiple_of(k * 128 + 128, 128), 128)
-        d = ext[16 : 16 + height, inner]
+        own = pl.ds(pl.multiple_of(k * 128 + 128, 128), 128)
+        d = ext[16 : 16 + height, own]
         e = res[:, lanes]
-        q = acc[:, inner] + damping * d
-        acc[:, inner] = q
+        q = acc[:, own] + damping * d
+        acc[:, own] = q
         terms = (e * e, d * q, e * q, q * q)
         return tuple(t + jnp.sum(v.reshape(-1, 8, 128), axis=0) for t, v in zip(carry, terms))
 
     zero = jnp.zeros((8, 128), jnp.float32)
     totals = lax.fori_loop(0, breadth // 128, sums, (zero,) * 4)
-    store = pltpu.make_async_copy(acc.at[:, 128 : 128 + breadth], applied_out, local_sem.at[2])
+    store = pltpu.make_async_copy(acc.at[:, 128 : 128 + breadth], applied_out, local_sem.at[len(places)])
     store.start()
 
     tile = jnp.zeros((8, 128), jnp.float32)
@@ -350,10 +416,21 @@
     store.wait()
 
 
+def update_kernel(scalars, iterate, residual, direction, applied, new_iterate, new_residual, new_direction):
+    step_length = scalars[0:1, 0:1]
+    ratio = scalars[1:2, 0:1]
+    d = direction[...]
+    new_iterate[...] = iterate[...] + step_length * d
+    rest = residual[...] - step_length * applied[...]
+    new_residual[...] = rest
+    new_direction[...] = rest + ratio * d
+
+
 def per_device(n_row, n_col, iterate, residual, direction, window_weight, freq_weight):
     height, breadth = direction.shape
     win_rows = height // 16
-    col, row, back, left, right = host_tables(win_rows)
+    chunks = breadth // 128 + 1
+    operands = (direction, residual, window_weight, freq_weight) + host_tables(win_rows)
     vmem = pl.BlockSpec(memory_space=pltpu.VMEM)
     hbm = pl.BlockSpec(memory_space=pl.ANY)
     dma = pltpu.SemaphoreType.DMA
@@ -361,20 +438,25 @@
     applied, scalars = pl.pallas_call(
         functools.partial(kernel, n_row, n_col),
         out_shape=(jax.ShapeDtypeStruct((height, breadth), f32), jax.ShapeDtypeStruct((8, 128), f32)),
-        in_specs=[hbm, hbm] + [vmem] * 10,
+        in_specs=[hbm] * len(operands),
         out_specs=(hbm, vmem),
-        scratch_shapes=[
+        scratch_shapes=[pltpu.VMEM(x.shape, x.dtype) for x in operands[2:]]
+        + [
+            pltpu.VMEM((768, 256), jnp.bfloat16),
+            pltpu.VMEM((768, 256), jnp.bfloat16),
             pltpu.VMEM((height + 32, breadth + 256), f32),
             pltpu.VMEM((height, breadth), f32),
             pltpu.VMEM((height, breadth + 256), f32),
+            pltpu.VMEM((chunks, height + 32, 256), jnp.bfloat16),
+            pltpu.VMEM((chunks, height + 32, 256), jnp.bfloat16),
             pltpu.VMEM((8, 128), f32),
             pltpu.VMEM((3, 8, 128), f32),
-            pltpu.VMEM((breadth // 128 + 1, 8, 128), f32),
+            pltpu.VMEM((chunks, 8, 128), f32),
             pltpu.VMEM((2, 32, 256), f32),
             pltpu.VMEM((n_col, 8, 128), f32),
             pltpu.VMEM((n_row, 8, 128), f32),
             pltpu.VMEM((8, 128), f32),
-            dma((3,)),
+            dma((len(operands) + 1,)),
             dma((8,)),
             dma((8,)),
             dma((3,)),
@@ -385,16 +467,19 @@
             dma((n_row,)),
         ],
         compiler_params=pltpu.CompilerParams(
-            collective_id=0, has_side_effects=True, vmem_limit_bytes=32 * 1024 * 1024
+            collective_id=0, has_side_effects=True, vmem_limit_bytes=60 * 1024 * 1024
         ),
         cost_estimate=pl.CostEstimate(flops=5_000_000_000, bytes_accessed=2_000_000, transcendentals=0),
-    )(direction, residual, window_weight, freq_weight, *col, *row, *back, left, right)
-    step_length = scalars[0:1, 0:1]
-    ratio = scalars[1:2, 0:1]
-    new_iterate = iterate + step_length * direction
-    new_residual = residual - step_length * applied
-    new_direction = new_residual + ratio * direction
-    return (new_iterate, new_residual, new_direction)
+    )(*operands)
+    block = pl.BlockSpec((height, 512), lambda i: (0, i))
+    return pl.pallas_call(
+        update_kernel,
+        grid=(breadth // 512,),
+        out_shape=(jax.ShapeDtypeStruct((height, breadth), f32),) * 3,
+        in_specs=[pl.BlockSpec((8, 128), lambda i: (0, 0))] + [block] * 4,
+        out_specs=(block,) * 3,
+        compiler_params=pltpu.CompilerParams(vmem_limit_bytes=60 * 1024 * 1024),
+    )(scalars, iterate, residual, direction, applied)
 
 
 def solution(mesh):

time: 44.5 us -> 31.3 us (0.70); the launches traced: 43.8 us -> 31.1 us
  local copies, waits for them, and re-layouts: 10.5 us -> 0 us
  other arithmetic: 2.52 us -> 0 us
    unnamed x26 -> x0, local copies, waits for them, and re-layouts: 9.95 us -> none
    pallas_call x0 -> x1, Pallas kernels: none -> 3.79 us  [per_device(): pl.pallas_call(update_kernel, grid=(breadth // 512,), out_shape=(jax.Shap...]
    pallas_call x1, Pallas kernels: 30.1 us -> 26.7 us  [per_device(): pl.pallas_call(functools.partial(kernel, n_row, n_col), out_shape=(jax.Sh...]
    add x1 -> x0, other arithmetic: 2.52 us -> none  [per_device(): new_direction = new_residual + ratio * direction]
    slice x1 -> x0, local copies, waits for them, and re-layouts: 0.58 us -> none  [per_device(): ratio = scalars[1:2, 0:1]]
where the time goes in v2:
time: 31.3 us; the launch traced here: 31.1 us
  Pallas kernels  30.5 us (97%)
  between operations  0.64 us (2%)
    pallas_call x1, Pallas kernels, per_device(): pl.pallas_call(functools.partial(kernel, n_row, n_col), out_shape=(jax.Sh...  26.7 us
    pallas_call x1, Pallas kernels, per_device(): pl.pallas_call(update_kernel, grid=(breadth // 512,), out_shape=(jax.Shap...  3.79 us

profile of v2, /device:TPU:0, one launch (start us, length us, event | category | flops | bytes accessed | tf_op | source)
XLA Modules:
  0.0 31.1 jit_solution(7299675404527852122)
XLA Ops:
  0.6 26.7 %shard_map.130 = (f32[64,2048]{1,0:T(8,128)}, f32[8,128]{1,0:T(8,128)}) custom-call(f32[64,2048]{1,0:T(8,128)} %direction.3, f32[64,2048]{1,0:T(8,128)} %residual.3, f32[4,128]{1,0:T(4,128)} %weight_in.1, f32[32,32]{1,0:T(8,128)} %freq_in.1, f32[256,256]{1,0:T(8,128)} %constant.12.clone.col_in, f32[256,256]{1,0:T(8,128)} %constant.13.clone.col_back_in, ...), custom_call_target="tpu_custom_call" | custom-call | flops 5000000000 | bytes 2000000 | tf_op jit(solution)/shard_map/pallas_call | solution.py:438
  27.3 3.8 %shard_map.131 = (f32[64,2048]{1,0:T(8,128)}, f32[64,2048]{1,0:T(8,128)}, f32[64,2048]{1,0:T(8,128)}) custom-call(f32[8,128]{1,0:T(8,128)} %get-tuple-element.5.scalars, f32[64,2048]{1,0:T(8,128)} %iterate.1, f32[64,2048]{1,0:T(8,128)} %residual.3, f32[64,2048]{1,0:T(8,128)} %direction.3, f32[64,2048]{1,0:T(8,128)} %get-tuple-element.6.applied), custom_call_target="tpu_custom_call" | custom-call | tf_op jit(solution)/shard_map/pallas_call | solution.py:475

commit v3 on v2

--- a/solution.py
+++ b/solution.py
@@ -52,7 +52,10 @@
     left = np.stack([even, -odd]).astype(np.float32)
     right = np.stack([np.repeat(even.T, 8, axis=1), np.repeat(odd.T, 8, axis=1)]).astype(np.float32)
     tables = (jnp.asarray(col, jnp.float32), jnp.asarray(col.T, jnp.float32))
-    tables = tables + (split_host(row, 1), split_host(row_back, 1))
+    rim = np.r_[0:32, height : height + 32]
+    rim_windows = np.r_[0:32, 32 * win_rows : 32 * win_rows + 32]
+    inside = row[32 : 32 * win_rows, 16 : 16 + height]
+    tables = tables + (split_host(inside, 1), split_host(row[rim_windows][:, rim], 1), split_host(row_back, 1))
     return tables + (jnp.asarray(left), jnp.asarray(right))
 
 
@@ -80,6 +83,7 @@
     col_in,
     col_back_in,
     row_in,
+    row_rim_in,
     row_back_in,
     left_in,
     right_in,
@@ -90,6 +94,7 @@
     col,
     col_back,
     row,
+    row_rim,
     row_back,
     left,
     right,
@@ -100,6 +105,11 @@
     acc,
     first_h,
     first_l,
+    mid_h,
+    mid_l,
+    row_b,
+    row_rim_b,
+    row_back_b,
     own_w,
     got_w,
     spread_w,
@@ -131,6 +141,7 @@
         (left_in, left),
         (right_in, right),
         (row_in, row),
+        (row_rim_in, row_rim),
         (residual, res),
         (row_back_in, row_back),
         (col_back_in, col_back),
@@ -204,18 +215,18 @@
             device_id_type=MESH,
         )
 
+    for i in range(3):
+
+        @pl.when(exists(*forward[i]))
+        def _(i=i):
+            weights(i).start()
+
     order = sorted(range(8), key=lambda i: around[i][1] != 0)
     for i in order:
 
         @pl.when(exists(*around[i]))
         def _(i=i):
             halo(i).start()
-
-    for i in range(3):
-
-        @pl.when(exists(*forward[i]))
-        def _(i=i):
-            weights(i).start()
 
     for i, (dr, dc) in enumerate(around):
 
@@ -257,18 +268,11 @@
             first_l[k, top:end, :] = l[at : at + end - top]
             at += end - top
 
-    inner = chunks - 2
-    group = 5 if inner % 5 == 0 else 1
-
-    def own_columns(g, carry):
-        columns([(1 + g * group + k, 16, 16 + height) for k in range(group)])
-        return carry
-
-    lax.fori_loop(0, inner // group, own_columns, 0)
-
     for i in range(3, len(fetches)):
         fetches[i].wait()
     stack_split(col_back, col_back3)
+    for table, cast in ((row, row_b), (row_rim, row_rim_b), (row_back, row_back_b)):
+        cast[...] = table[...].astype(jnp.bfloat16)
     for m in range(2):
         folded = jnp.dot(left[m], freq[...], precision=lax.Precision.HIGHEST, preferred_element_type=jnp.float32)
         mix[m] = jnp.dot(folded, right[m], precision=lax.Precision.HIGHEST, preferred_element_type=jnp.float32)
@@ -298,32 +302,58 @@
             x = x + pltpu.roll(x, step, 1)
         spread_w[k] = x
 
+    even = mix[0]
+    odd = mix[1]
+
+    def weigh(coef, k, windows):
+        pieces = []
+        for i, a in enumerate(windows):
+            z = coef[32 * i : 32 * i + 32]
+            swapped = jnp.concatenate([z[16:], z[:16]], axis=0)
+            swapped = jnp.concatenate([swapped[:, 128:], swapped[:, :128]], axis=1)
+            w = spread_w[k, a : a + 1, :]
+            pieces.append((even * z + odd * swapped) * jnp.concatenate([w, w], axis=1))
+        return split(jnp.concatenate(pieces, axis=0))
+
+    def inside_windows(k):
+        coef = dot(row_b[...], thrice(first_h[k, 16 : 16 + height], first_l[k, 16 : 16 + height], 0))
+        h, l = weigh(coef, k, range(1, win_rows))
+        mid_h[k] = h
+        mid_l[k] = l
+
+    inner = chunks - 2
+    group = 5 if inner % 5 == 0 else 1
+
+    def own_columns(g, carry):
+        ks = [1 + g * group + k for k in range(group)]
+        columns([(k, 16, 16 + height) for k in ks])
+        for k in ks:
+            inside_windows(k)
+        return carry
+
+    lax.fori_loop(0, inner // group, own_columns, 0)
+
     for i in range(8):
         dr, dc = around[i]
 
         @pl.when(exists(-dr, -dc))
         def _(i=i):
             halo(i).wait_recv()
-
-    even = mix[0]
-    odd = mix[1]
 
     rim = [(0, 0, height + 32), (chunks - 1, 0, height + 32)]
     for k in range(1, chunks - 1):
         rim += [(k, 0, 16), (k, 16 + height, 32 + height)]
     columns(rim)
+    inside_windows(0)
+    inside_windows(chunks - 1)
 
     def rows_of(k):
-        coef = dot(row[...].astype(jnp.bfloat16), thrice(first_h[k], first_l[k], 0))
-        pieces = []
-        for a in range(win_rows + 1):
-            z = coef[32 * a : 32 * a + 32]
-            swapped = jnp.concatenate([z[16:], z[:16]], axis=0)
-            swapped = jnp.concatenate([swapped[:, 128:], swapped[:, :128]], axis=1)
-            w = spread_w[k, a : a + 1, :]
-            pieces.append((even * z + odd * swapped) * jnp.concatenate([w, w], axis=1))
-        h, l = split(jnp.concatenate(pieces, axis=0))
-        return split(dot(row_back[...].astype(jnp.bfloat16), thrice(h, l, 0)))
+        h, l = (jnp.concatenate([x[k, 0:32], x[k, height : height + 32]], axis=0) for x in (first_h, first_l))
+        coef = dot(row_rim_b[...], thrice(h, l, 0))
+        h, l = weigh(coef, k, (0, win_rows))
+        h = jnp.concatenate([h[:32], mid_h[k], h[32:]], axis=0)
+        l = jnp.concatenate([l[:32], mid_l[k], l[32:]], axis=0)
+        return split(dot(row_back_b[...], thrice(h, l, 0)))
 
     def chunk_group(ks):
         parts = [rows_of(k) for k in ks]
@@ -416,14 +446,35 @@
     store.wait()
 
 
-def update_kernel(scalars, iterate, residual, direction, applied, new_iterate, new_residual, new_direction):
+def update_kernel(
+    scalars, iterate, residual, direction, applied, new_iterate, new_residual, new_direction, held, made, sem_in, sem_out
+):
+    parts = 4
+    rows = iterate.shape[0] // parts
+    fetches, stores = [], []
+    for p in range(parts):
+        here = pl.ds(p * rows, rows)
+        for i, x in enumerate((direction, iterate, residual, applied)):
+            fetches.append(pltpu.make_async_copy(x.at[here], held.at[i, here], sem_in.at[p, i]))
+        for i, x in enumerate((new_iterate, new_residual, new_direction)):
+            stores.append(pltpu.make_async_copy(made.at[i, here], x.at[here], sem_out.at[p, i]))
+    for fetch in fetches:
+        fetch.start()
     step_length = scalars[0:1, 0:1]
     ratio = scalars[1:2, 0:1]
-    d = direction[...]
-    new_iterate[...] = iterate[...] + step_length * d
-    rest = residual[...] - step_length * applied[...]
-    new_residual[...] = rest
-    new_direction[...] = rest + ratio * d
+    for p in range(parts):
+        here = pl.ds(p * rows, rows)
+        for fetch in fetches[4 * p : 4 * p + 4]:
+            fetch.wait()
+        d = held[0, here]
+        made[0, here] = held[1, here] + step_length * d
+        rest = held[2, here] - step_length * held[3, here]
+        made[1, here] = rest
+        made[2, here] = rest + ratio * d
+        for store in stores[3 * p : 3 * p + 3]:
+            store.start()
+    for store in stores:
+        store.wait()
 
 
 def per_device(n_row, n_col, iterate, residual, direction, window_weight, freq_weight):
@@ -449,6 +500,11 @@
             pltpu.VMEM((height, breadth + 256), f32),
             pltpu.VMEM((chunks, height + 32, 256), jnp.bfloat16),
             pltpu.VMEM((chunks, height + 32, 256), jnp.bfloat16),
+            pltpu.VMEM((chunks, 32 * (win_rows - 1), 256), jnp.bfloat16),
+            pltpu.VMEM((chunks, 32 * (win_rows - 1), 256), jnp.bfloat16),
+        ]
+        + [pltpu.VMEM(x.shape, jnp.bfloat16) for x in operands[6:9]]
+        + [
             pltpu.VMEM((8, 128), f32),
             pltpu.VMEM((3, 8, 128), f32),
             pltpu.VMEM((chunks, 8, 128), f32),
@@ -471,13 +527,17 @@
         ),
         cost_estimate=pl.CostEstimate(flops=5_000_000_000, bytes_accessed=2_000_000, transcendentals=0),
     )(*operands)
-    block = pl.BlockSpec((height, 512), lambda i: (0, i))
     return pl.pallas_call(
         update_kernel,
-        grid=(breadth // 512,),
         out_shape=(jax.ShapeDtypeStruct((height, breadth), f32),) * 3,
-        in_specs=[pl.BlockSpec((8, 128), lambda i: (0, 0))] + [block] * 4,
-        out_specs=(block,) * 3,
+        in_specs=[vmem] + [hbm] * 4,
+        out_specs=(hbm,) * 3,
+        scratch_shapes=[
+            pltpu.VMEM((4, height, breadth), f32),
+            pltpu.VMEM((3, height, breadth), f32),
+            dma((4, 4)),
+            dma((4, 3)),
+        ],
         compiler_params=pltpu.CompilerParams(vmem_limit_bytes=60 * 1024 * 1024),
     )(scalars, iterate, residual, direction, applied)
 

time: 31.3 us -> 28 us (0.89)
  Pallas kernels: 30.5 us -> 27.1 us
    pallas_call x1, Pallas kernels: 26.7 us -> 23.8 us  [per_device(): pl.pallas_call(functools.partial(kernel, n_row, n_col), out_shape=(jax.Sh...]
    pallas_call x1, Pallas kernels: 3.79 us -> 3.29 us  [per_device(): pl.pallas_call(update_kernel, out_shape=(jax.ShapeDtypeStruct((height, br...]
where the time goes in v3:
time: 28 us; the launch traced here: 27.8 us
  Pallas kernels  27.1 us (97%)
  between operations  0.64 us (2%)
    pallas_call x1, Pallas kernels, per_device(): pl.pallas_call(functools.partial(kernel, n_row, n_col), out_shape=(jax.Sh...  23.8 us
    pallas_call x1, Pallas kernels, per_device(): pl.pallas_call(update_kernel, out_shape=(jax.ShapeDtypeStruct((height, br...  3.29 us

profile of v3, /device:TPU:0, one launch (start us, length us, event | category | flops | bytes accessed | tf_op | source)
XLA Modules:
  0.0 27.8 jit_solution(8333330136480928139)
XLA Ops:
  0.6 23.8 %shard_map.139 = (f32[64,2048]{1,0:T(8,128)}, f32[8,128]{1,0:T(8,128)}) custom-call(f32[64,2048]{1,0:T(8,128)} %direction.3, f32[64,2048]{1,0:T(8,128)} %residual.3, f32[4,128]{1,0:T(4,128)} %weight_in.1, f32[32,32]{1,0:T(8,128)} %freq_in.1, f32[256,256]{1,0:T(8,128)} %constant.14.clone.col_in, f32[256,256]{1,0:T(8,128)} %constant.15.clone.col_back_in, ...), custom_call_target="tpu_custom_call" | custom-call | flops 5000000000 | bytes 2000000 | tf_op jit(solution)/shard_map/pallas_call | solution.py:489
  24.5 3.3 %shard_map.140 = (f32[64,2048]{1,0:T(8,128)}, f32[64,2048]{1,0:T(8,128)}, f32[64,2048]{1,0:T(8,128)}) custom-call(f32[8,128]{1,0:T(8,128)} %get-tuple-element.5.scalars, f32[64,2048]{1,0:T(8,128)} %iterate.1, f32[64,2048]{1,0:T(8,128)} %residual.3, f32[64,2048]{1,0:T(8,128)} %direction.3, f32[64,2048]{1,0:T(8,128)} %get-tuple-element.6.applied), custom_call_target="tpu_custom_call" | custom-call | tf_op jit(solution)/shard_map/pallas_call | solution.py:530

commit v4 on v3

--- a/solution.py
+++ b/solution.py
@@ -331,7 +331,8 @@
             inside_windows(k)
         return carry
 
-    lax.fori_loop(0, inner // group, own_columns, 0)
+    for g in range(inner // group):
+        own_columns(g, 0)
 
     for i in range(8):
         dr, dc = around[i]
@@ -368,13 +369,14 @@
         chunk_group([g * group + k for k in range(group)])
         return carry
 
-    lax.fori_loop(0, chunks // group, body, 0)
+    for g in range(chunks // group):
+        body(g, 0)
     if chunks % group:
         chunk_group(list(range(chunks - chunks % group, chunks)))
 
     def sums(k, carry):
-        lanes = pl.ds(pl.multiple_of(k * 128, 128), 128)
-        own = pl.ds(pl.multiple_of(k * 128 + 128, 128), 128)
+        lanes = pl.ds(k * 128, 128)
+        own = pl.ds(k * 128 + 128, 128)
         d = ext[16 : 16 + height, own]
         e = res[:, lanes]
         q = acc[:, own] + damping * d
@@ -383,7 +385,9 @@
         return tuple(t + jnp.sum(v.reshape(-1, 8, 128), axis=0) for t, v in zip(carry, terms))
 
     zero = jnp.zeros((8, 128), jnp.float32)
-    totals = lax.fori_loop(0, breadth // 128, sums, (zero,) * 4)
+    totals = (zero,) * 4
+    for k in range(breadth // 128):
+        totals = sums(k, totals)
     store = pltpu.make_async_copy(acc.at[:, 128 : 128 + breadth], applied_out, local_sem.at[len(places)])
     store.start()
 

time: 28 us -> 27.6 us (0.986)
  Pallas kernels: 27.1 us -> 26.7 us
    pallas_call x1, Pallas kernels: 23.8 us -> 23.4 us  [per_device(): pl.pallas_call(functools.partial(kernel, n_row, n_col), out_shape=(jax.Sh...]
where the time goes in v4:
time: 27.6 us; the launch traced here: 27.3 us
  Pallas kernels  26.7 us (97%)
  between operations  0.64 us (2%)
    pallas_call x1, Pallas kernels, per_device(): pl.pallas_call(functools.partial(kernel, n_row, n_col), out_shape=(jax.Sh...  23.4 us
    pallas_call x1, Pallas kernels, per_device(): pl.pallas_call(update_kernel, out_shape=(jax.ShapeDtypeStruct((height, br...  3.29 us

profile of v4, /device:TPU:0, one launch (start us, length us, event | category | flops | bytes accessed | tf_op | source)
XLA Modules:
  0.0 27.3 jit_solution(3516053629824714259)
XLA Ops:
  0.6 23.4 %shard_map.139 = (f32[64,2048]{1,0:T(8,128)}, f32[8,128]{1,0:T(8,128)}) custom-call(f32[64,2048]{1,0:T(8,128)} %direction.3, f32[64,2048]{1,0:T(8,128)} %residual.3, f32[4,128]{1,0:T(4,128)} %weight_in.1, f32[32,32]{1,0:T(8,128)} %freq_in.1, f32[256,256]{1,0:T(8,128)} %constant.14.clone.col_in, f32[256,256]{1,0:T(8,128)} %constant.15.clone.col_back_in, ...), custom_call_target="tpu_custom_call" | custom-call | flops 5000000000 | bytes 2000000 | tf_op jit(solution)/shard_map/pallas_call | solution.py:493
  24.1 3.3 %shard_map.140 = (f32[64,2048]{1,0:T(8,128)}, f32[64,2048]{1,0:T(8,128)}, f32[64,2048]{1,0:T(8,128)}) custom-call(f32[8,128]{1,0:T(8,128)} %get-tuple-element.5.scalars, f32[64,2048]{1,0:T(8,128)} %iterate.1, f32[64,2048]{1,0:T(8,128)} %residual.3, f32[64,2048]{1,0:T(8,128)} %direction.3, f32[64,2048]{1,0:T(8,128)} %get-tuple-element.6.applied), custom_call_target="tpu_custom_call" | custom-call | tf_op jit(solution)/shard_map/pallas_call | solution.py:534

commit v5 on v4

--- a/solution.py
+++ b/solution.py
@@ -268,6 +268,11 @@
             first_l[k, top:end, :] = l[at : at + end - top]
             at += end - top
 
+    inner = chunks - 2
+    group = 5 if inner % 5 == 0 else 1
+    for g in range(inner // group):
+        columns([(1 + g * group + k, 16, 16 + height) for k in range(group)])
+
     for i in range(3, len(fetches)):
         fetches[i].wait()
     stack_split(col_back, col_back3)
@@ -321,18 +326,14 @@
         mid_h[k] = h
         mid_l[k] = l
 
-    inner = chunks - 2
-    group = 5 if inner % 5 == 0 else 1
-
-    def own_columns(g, carry):
+    def own_windows(g, carry):
         ks = [1 + g * group + k for k in range(group)]
-        columns([(k, 16, 16 + height) for k in ks])
         for k in ks:
             inside_windows(k)
         return carry
 
     for g in range(inner // group):
-        own_columns(g, 0)
+        own_windows(g, 0)
 
     for i in range(8):
         dr, dc = around[i]

time: 27.6 us -> 26.5 us (0.960)
  Pallas kernels: 26.7 us -> 25.6 us
    pallas_call x1, Pallas kernels: 23.4 us -> 22.3 us  [per_device(): pl.pallas_call(functools.partial(kernel, n_row, n_col), out_shape=(jax.Sh...]
where the time goes in v5:
time: 26.5 us; the launch traced here: 26.3 us
  Pallas kernels  25.6 us (97%)
  between operations  0.64 us (2%)
    pallas_call x1, Pallas kernels, per_device(): pl.pallas_call(functools.partial(kernel, n_row, n_col), out_shape=(jax.Sh...  22.3 us
    pallas_call x1, Pallas kernels, per_device(): pl.pallas_call(update_kernel, out_shape=(jax.ShapeDtypeStruct((height, br...  3.29 us

profile of v5, /device:TPU:0, one launch (start us, length us, event | category | flops | bytes accessed | tf_op | source)
XLA Modules:
  0.0 26.3 jit_solution(9633080272101290679)
XLA Ops:
  0.6 22.3 %shard_map.139 = (f32[64,2048]{1,0:T(8,128)}, f32[8,128]{1,0:T(8,128)}) custom-call(f32[64,2048]{1,0:T(8,128)} %direction.3, f32[64,2048]{1,0:T(8,128)} %residual.3, f32[4,128]{1,0:T(4,128)} %weight_in.1, f32[32,32]{1,0:T(8,128)} %freq_in.1, f32[256,256]{1,0:T(8,128)} %constant.14.clone.col_in, f32[256,256]{1,0:T(8,128)} %constant.15.clone.col_back_in, ...), custom_call_target="tpu_custom_call" | custom-call | flops 5000000000 | bytes 2000000 | tf_op jit(solution)/shard_map/pallas_call | solution.py:494
  23.0 3.3 %shard_map.140 = (f32[64,2048]{1,0:T(8,128)}, f32[64,2048]{1,0:T(8,128)}, f32[64,2048]{1,0:T(8,128)}) custom-call(f32[8,128]{1,0:T(8,128)} %get-tuple-element.5.scalars, f32[64,2048]{1,0:T(8,128)} %iterate.1, f32[64,2048]{1,0:T(8,128)} %residual.3, f32[64,2048]{1,0:T(8,128)} %direction.3, f32[64,2048]{1,0:T(8,128)} %get-tuple-element.6.applied), custom_call_target="tpu_custom_call" | custom-call | tf_op jit(solution)/shard_map/pallas_call | solution.py:535
